TPU v7x, 32 devices: a whole 2x2x4 slice. The times are simulated.
32 devices in a mesh: pipe: 2 (over x), expert: 8 (over z, y), dp: 2 (over core).
Axes of the slice: x: 2, y: 2, z: 4, core: 2. Of those that a mesh axis runs over, the one named last changes fastest.
Arguments:
- saved: bfloat16 [1, 2, 2048, 2560], P(None, 'pipe', ('expert', 'dp')), may hold values from -6 to 6
- cotangent: bfloat16 [2048, 2560], P(('expert', 'dp'), 'pipe'), may hold values from -1.1953125 to 1.1953125
- routes: int32 [1, 2, 2048, 1], P(None, 'pipe', ('expert', 'dp')), may hold values from 0 to 1; in each aligned block of 16 rows (0 to 15, 16 to 31, ..., all dimensions but the last counted through in order) at most 8 rows name the same one
- w_gate: bfloat16 [1, 2, 2048, 2560], P(None, 'pipe', 'expert', 'dp'), may hold values from -0.125 to 0.125
- w_up: bfloat16 [1, 2, 2048, 2560], P(None, 'pipe', 'expert', 'dp'), may hold values from -0.125 to 0.125
- w_down: bfloat16 [1, 2, 2048, 2560], P(None, 'pipe', 'expert', 'dp'), may hold values from -0.0625 to 0.0625
Outputs:
- grad_gate: bfloat16 [1, 2, 2048, 2560], P(None, 'pipe', 'expert', 'dp')
- grad_up: bfloat16 [1, 2, 2048, 2560], P(None, 'pipe', 'expert', 'dp')
Inputs may be any that keep to these rules, and one draw needn't show every extreme that they name: In each aligned block of 16 rows of routes (one micro-batch of one device, rows taken in order over all leading dimensions) no expert is named more than 8 times.
All inputs are finite; a program needn't handle non-finite values.
Results may differ from a plain program's by a relative error of at most 0.017.
Values may be sent and summed in bfloat16 or wider, within the bound.
A program may use at most 64 MiB of HBM per device.

v0:
```python
import jax
import jax.numpy as jnp
from jax import lax
from jax.sharding import PartitionSpec as P

GROUP = 4
MICRO = 8


epsilon = 1e-06


def shifted(block, axis, distance):
    devices = range(lax.axis_size(axis))
    route = [(i - distance, i) for i in devices if i - distance in devices]
    return lax.ppermute(block, axis, route)


def slot_tables(route_ids, experts, capacity):
    onehot = (route_ids[..., None] == jnp.arange(experts, dtype=jnp.int32)).astype(jnp.int32)
    ranking = jnp.sum((jnp.cumsum(onehot, axis=2) - onehot) * onehot, axis=3)
    slot_ids = route_ids * capacity + ranking
    positions = jnp.arange(experts * capacity, dtype=jnp.int32)[:, None]
    placing = (slot_ids[..., None, :] == positions).astype(jnp.bfloat16)
    return (placing, slot_ids)


def shards(saved, cotangent, routes, w_gate, w_up, w_down):
    sections = lax.axis_size("pipe")
    width_all = lax.axis_size("expert")
    section_index = lax.axis_index("pipe")
    stretches = saved.shape[0]
    tok_dev = saved.shape[2]
    tok_mb = tok_dev // MICRO
    experts = width_all // GROUP
    capacity = max(2, tok_mb // experts)
    period = sections + MICRO - 1
    slot_count = width_all * capacity
    head_grad = lax.all_gather(cotangent, "pipe", axis=1, tiled=True)
    feature_count = head_grad.shape[1]
    slabs = (
        lax.all_gather(w_gate, "dp", axis=3, tiled=True),
        lax.all_gather(w_up, "dp", axis=3, tiled=True),
        lax.all_gather(w_down, "dp", axis=3, tiled=True),
    )
    gate_w = slabs[0][:, 0]
    up_w = slabs[1][:, 0]
    down_w = slabs[2][:, 0]
    hidden = gate_w.shape[1]
    inputs_f = saved[:, 0].astype(jnp.float32).reshape(stretches, MICRO, tok_mb, feature_count)
    norm_scale = lax.rsqrt(jnp.mean(inputs_f * inputs_f, axis=3, keepdims=True) + epsilon)
    unit_f = inputs_f * norm_scale
    unit_b = unit_f.astype(jnp.bfloat16)
    route_ids = routes[:, 0, :, 0].reshape(stretches, MICRO, tok_mb)
    placing, slot_ids = slot_tables(route_ids, experts, capacity)
    unit_slots = jnp.einsum("vmst,vmtd->vmsd", placing, unit_b, preferred_element_type=jnp.float32)
    unit_slots = unit_slots.astype(jnp.bfloat16).reshape(
        stretches, MICRO, experts, capacity, feature_count
    )
    unit_send = jnp.repeat(unit_slots, GROUP, axis=2)
    unit_recv = lax.all_to_all(unit_send, "expert", split_axis=2, concat_axis=2, tiled=True)
    unit_rows = unit_recv.reshape(stretches, MICRO, slot_count, feature_count)
    gate_ahead = jnp.einsum("vmrd,vhd->vmrh", unit_rows, gate_w, preferred_element_type=jnp.float32)
    up_ahead = jnp.einsum("vmrd,vhd->vmrh", unit_rows, up_w, preferred_element_type=jnp.float32)
    top_section = section_index == sections - 1

    def tick_step(tick_index, loop_state):
        carried, gate_store, up_store = loop_state
        stretch_index = 0
        micro_raw = tick_index - (sections - 1 - section_index)
        active = (micro_raw >= 0) & (micro_raw < MICRO)
        micro_index = jnp.clip(micro_raw, 0, MICRO - 1)
        seed_rows = lax.dynamic_slice_in_dim(head_grad, micro_index * tok_mb, tok_mb, 0)
        grad_in = jnp.where(top_section, seed_rows, carried)
        grad_in = jnp.where(active, grad_in, jnp.zeros_like(grad_in))
        place_now = placing[stretch_index, micro_index].reshape(experts, capacity, tok_mb)
        slot_grads = jnp.einsum(
            "ect,td->ecd", place_now, grad_in, preferred_element_type=jnp.float32
        )
        sending = jnp.repeat(slot_grads.astype(jnp.bfloat16), GROUP, axis=0)
        grad_rows = lax.all_to_all(
            sending, "expert", split_axis=0, concat_axis=0, tiled=True
        ).reshape(slot_count, feature_count)
        gate_slab = gate_w[stretch_index]
        up_slab = up_w[stretch_index]
        down_slab = down_w[stretch_index]
        gate = gate_ahead[stretch_index, micro_index]
        up = up_ahead[stretch_index, micro_index]
        hidden_grad = jnp.einsum(
            "rd,hd->rh", grad_rows, down_slab, preferred_element_type=jnp.float32
        )
        sigmoid_gate = jax.nn.sigmoid(gate)
        gate_grad = (hidden_grad * up * sigmoid_gate * (1.0 + gate * (1.0 - sigmoid_gate))).astype(
            jnp.bfloat16
        )
        up_grad = (hidden_grad * gate * sigmoid_gate).astype(jnp.bfloat16)
        partial_value = jnp.dot(gate_grad, gate_slab, preferred_element_type=jnp.float32)
        partial_value = (
            partial_value + jnp.dot(up_grad, up_slab, preferred_element_type=jnp.float32)
        ).astype(jnp.bfloat16)
        returned = lax.all_to_all(
            partial_value.reshape(width_all, capacity, feature_count),
            "expert",
            split_axis=0,
            concat_axis=0,
            tiled=True,
        )
        summed = (
            returned.reshape(experts, GROUP, capacity, feature_count)
            .astype(jnp.float32)
            .sum(axis=1)
        )
        unit_grad = jnp.take(
            summed.reshape(experts * capacity, feature_count),
            slot_ids[stretch_index, micro_index],
            axis=0,
        )
        unit_here = unit_f[stretch_index, micro_index]
        scale_rows = norm_scale[stretch_index, micro_index]
        norm_grad = scale_rows * (
            unit_grad - unit_here * jnp.mean(unit_grad * unit_here, axis=1, keepdims=True)
        )
        grad_out = (grad_in.astype(jnp.float32) + norm_grad).astype(jnp.bfloat16)
        carried = shifted(grad_out, "pipe", -1)
        gate_store = jnp.where(
            active, gate_store.at[stretch_index, micro_index].set(gate_grad), gate_store
        )
        up_store = jnp.where(active, up_store.at[stretch_index, micro_index].set(up_grad), up_store)
        return (carried, gate_store, up_store)

    start_state = (
        jnp.zeros((tok_mb, feature_count), jnp.bfloat16),
        jnp.zeros((stretches, MICRO, slot_count, hidden), jnp.bfloat16),
        jnp.zeros((stretches, MICRO, slot_count, hidden), jnp.bfloat16),
    )
    final_state = lax.fori_loop(0, period, tick_step, start_state)
    flat_units = unit_rows.reshape(stretches, MICRO * slot_count, feature_count)
    part_gate = jnp.einsum(
        "vrh,vrd->vhd",
        final_state[1].reshape(stretches, MICRO * slot_count, hidden),
        flat_units,
        preferred_element_type=jnp.float32,
    )
    part_up = jnp.einsum(
        "vrh,vrd->vhd",
        final_state[2].reshape(stretches, MICRO * slot_count, hidden),
        flat_units,
        preferred_element_type=jnp.float32,
    )
    totals = (
        lax.psum_scatter(
            part_gate.astype(jnp.bfloat16), "dp", scatter_dimension=2, tiled=True
        ).astype(jnp.float32),
        lax.psum_scatter(
            part_up.astype(jnp.bfloat16), "dp", scatter_dimension=2, tiled=True
        ).astype(jnp.float32),
    )
    grad_gate = totals[0].astype(jnp.bfloat16)[:, None]
    grad_up = totals[1].astype(jnp.bfloat16)[:, None]
    return (grad_gate, grad_up)


def solution(mesh):
    in_specs = (
        P(None, "pipe", ("expert", "dp"), None),
        P(("expert", "dp"), "pipe"),
        P(None, "pipe", ("expert", "dp"), None),
        P(None, "pipe", "expert", "dp"),
        P(None, "pipe", "expert", "dp"),
        P(None, "pipe", "expert", "dp"),
    )
    out_specs = (P(None, "pipe", "expert", "dp"), P(None, "pipe", "expert", "dp"))
    return jax.shard_map(shards, mesh=mesh, in_specs=in_specs, out_specs=out_specs, check_vma=False)
```

profile of v0, /device:TPU:1, one launch (start us, length us, event | category | flops | bytes accessed | tf_op | source)
XLA Modules:
  0.0 489.6 jit_solution(13634994165569149674)
XLA Ops:
  13.8 6.4 %all-to-all-start.2 = ((bf16[1,8,8,8,2560]{4,3,1,0,2:T(8,128)(2,1)}), bf16[1,8,8,8,2560]{4,3,1,0,2:T(8,128)(2,1)}, u32[]{:S(2)}, u32[]{:S(2)}) async-start(bf16[1,8,8,8,2560]{4,3,1,0,2:T(8,128)(2,1)} %bitcast.184), calls=%async_computation.2 | async-start | bytes 5242880 | tf_op jit(solution)/shard_map/all_to_all | solution.py:61
  22.6 9.0 %all_gather.12 = bf16[128,2560]{1,0:T(8,128)(2,1)} all-gather(bf16[128,1280]{1,0:T(8,128)(2,1)S(1)} %copy-done.3), channel_id=1, replica_groups=mesh['pipe'=2,'expert'=8,'dp'=2] {'pipe'}, dimensions={1}, use_global_device_ids=true | all-gather | bytes 983040 | tf_op jit(solution)/shard_map/all_gather | solution.py:39
  32.9 46.0 %all-to-all-done.2 = bf16[1,8,8,8,2560]{4,3,1,0,2:T(8,128)(2,1)} async-done(((bf16[1,8,8,8,2560]{4,3,1,0,2:T(8,128)(2,1)}), bf16[1,8,8,8,2560]{4,3,1,0,2:T(8,128)(2,1)}, u32[]{:S(2)}, u32[]{:S(2)}) %all-to-all-start.2) | async-done | bytes 2621472 | tf_op jit(solution)/shard_map/all_to_all | solution.py:61
  78.9 3.5 copy.31
  82.4 3.8 fusion.40
  86.2 3.9 fusion.45
  90.9 342.8 %while.21 = (s32[]{:T(128)}, bf16[16,2560]{1,0:T(8,128)(2,1)S(1)}, bf16[1,8,64,256]{3,2,1,0:T(8,128)(2,1)S(1)}, bf16[1,8,64,256]{3,2,1,0:T(8,128)(2,1)}, s32[]{:...) while((s32[]{:T(128)}, bf16[16,2560]{1,0:T(8,128)(2,1)S(1)}, ...), condition=%wide.region_7.8_spmd, body=%wide.region_3.7_spmd.sunk | while | flops 254477488 | bytes 10972429 | solution.py:136
  92.7 4.7 all-to-all-start
  98.1 7.7 %all-to-all-done = bf16[8,8,2560]{2,1,0:T(8,128)(2,1)S(1)} async-done(((bf16[8,8,2560]{2,1,0:T(8,128)(2,1)}), bf16[8,8,2560]{2,1,0:T(8,128)(2,1)S(1)}, u32[]{:S(2)}, u32[]{:S(2)}) %all-to-all-start) | async-done | bytes 327712 | tf_op jit(solution)/shard_map/while/body/eval_jaxpr/all_to_all | solution.py:81
  110.4 5.4 %all-to-all-start.1 = ((bf16[8,8,2560]{2,1,0:T(8,128)(2,1)}), bf16[8,8,2560]{2,1,0:T(8,128)(2,1)S(1)}, u32[]{:S(2)}, u32[]{:S(2)}) async-start(bf16[8,8,2560]{2,1,0:T(8,128)(2,1)} %fusion.89), calls=%async_computation.1 | async-start | bytes 655360 | tf_op jit(solution)/shard_map/while/body/eval_jaxpr/all_to_all | solution.py:101
  115.8 8.1 %all-to-all-done.1 = bf16[8,8,2560]{2,1,0:T(8,128)(2,1)S(1)} async-done(((bf16[8,8,2560]{2,1,0:T(8,128)(2,1)}), bf16[8,8,2560]{2,1,0:T(8,128)(2,1)S(1)}, u32[]{:S(2)}, u32[]{:S(2)}) %all-to-all-start.1) | async-done | bytes 327712 | tf_op jit(solution)/shard_map/while/body/eval_jaxpr/all_to_all | solution.py:101
  128.0 3.9 collective-permute-done
  133.7 5.4 %all-to-all-start = ((bf16[8,8,2560]{2,1,0:T(8,128)(2,1)}), bf16[8,8,2560]{2,1,0:T(8,128)(2,1)S(1)}, u32[]{:S(2)}, u32[]{:S(2)}) async-start(bf16[8,8,2560]{2,1,0:T(8,128)(2,1)} %bitcast.177), calls=%async_computation | async-start | bytes 655360 | tf_op jit(solution)/shard_map/while/body/eval_jaxpr/all_to_all | solution.py:81
  139.8 6.9 %all-to-all-done = bf16[8,8,2560]{2,1,0:T(8,128)(2,1)S(1)} async-done(((bf16[8,8,2560]{2,1,0:T(8,128)(2,1)}), bf16[8,8,2560]{2,1,0:T(8,128)(2,1)S(1)}, u32[]{:S(2)}, u32[]{:S(2)}) %all-to-all-start) | async-done | bytes 327712 | tf_op jit(solution)/shard_map/while/body/eval_jaxpr/all_to_all | solution.py:81
  151.2 5.0 %all-to-all-start.1 = ((bf16[8,8,2560]{2,1,0:T(8,128)(2,1)}), bf16[8,8,2560]{2,1,0:T(8,128)(2,1)S(1)}, u32[]{:S(2)}, u32[]{:S(2)}) async-start(bf16[8,8,2560]{2,1,0:T(8,128)(2,1)} %fusion.89), calls=%async_computation.1 | async-start | bytes 655360 | tf_op jit(solution)/shard_map/while/body/eval_jaxpr/all_to_all | solution.py:101
  156.3 7.5 %all-to-all-done.1 = bf16[8,8,2560]{2,1,0:T(8,128)(2,1)S(1)} async-done(((bf16[8,8,2560]{2,1,0:T(8,128)(2,1)}), bf16[8,8,2560]{2,1,0:T(8,128)(2,1)S(1)}, u32[]{:S(2)}, u32[]{:S(2)}) %all-to-all-start.1) | async-done | bytes 327712 | tf_op jit(solution)/shard_map/while/body/eval_jaxpr/all_to_all | solution.py:101
  168.0 3.9 collective-permute-done
  173.6 5.5 %all-to-all-start = ((bf16[8,8,2560]{2,1,0:T(8,128)(2,1)}), bf16[8,8,2560]{2,1,0:T(8,128)(2,1)S(1)}, u32[]{:S(2)}, u32[]{:S(2)}) async-start(bf16[8,8,2560]{2,1,0:T(8,128)(2,1)} %bitcast.177), calls=%async_computation | async-start | bytes 655360 | tf_op jit(solution)/shard_map/while/body/eval_jaxpr/all_to_all | solution.py:81
  179.9 6.8 %all-to-all-done = bf16[8,8,2560]{2,1,0:T(8,128)(2,1)S(1)} async-done(((bf16[8,8,2560]{2,1,0:T(8,128)(2,1)}), bf16[8,8,2560]{2,1,0:T(8,128)(2,1)S(1)}, u32[]{:S(2)}, u32[]{:S(2)}) %all-to-all-start) | async-done | bytes 327712 | tf_op jit(solution)/shard_map/while/body/eval_jaxpr/all_to_all | solution.py:81
  191.3 4.1 all-to-all-start.1
  195.4 7.5 %all-to-all-done.1 = bf16[8,8,2560]{2,1,0:T(8,128)(2,1)S(1)} async-done(((bf16[8,8,2560]{2,1,0:T(8,128)(2,1)}), bf16[8,8,2560]{2,1,0:T(8,128)(2,1)S(1)}, u32[]{:S(2)}, u32[]{:S(2)}) %all-to-all-start.1) | async-done | bytes 327712 | tf_op jit(solution)/shard_map/while/body/eval_jaxpr/all_to_all | solution.py:101
  207.1 3.9 collective-permute-done
  212.8 3.4 all-to-all-start
  216.9 6.7 %all-to-all-done = bf16[8,8,2560]{2,1,0:T(8,128)(2,1)S(1)} async-done(((bf16[8,8,2560]{2,1,0:T(8,128)(2,1)}), bf16[8,8,2560]{2,1,0:T(8,128)(2,1)S(1)}, u32[]{:S(2)}, u32[]{:S(2)}) %all-to-all-start) | async-done | bytes 327712 | tf_op jit(solution)/shard_map/while/body/eval_jaxpr/all_to_all | solution.py:81
  228.2 3.4 all-to-all-start.1
  231.7 7.4 %all-to-all-done.1 = bf16[8,8,2560]{2,1,0:T(8,128)(2,1)S(1)} async-done(((bf16[8,8,2560]{2,1,0:T(8,128)(2,1)}), bf16[8,8,2560]{2,1,0:T(8,128)(2,1)S(1)}, u32[]{:S(2)}, u32[]{:S(2)}) %all-to-all-start.1) | async-done | bytes 327712 | tf_op jit(solution)/shard_map/while/body/eval_jaxpr/all_to_all | solution.py:101
  243.3 3.9 collective-permute-done
  248.9 3.4 all-to-all-start
  253.1 6.7 %all-to-all-done = bf16[8,8,2560]{2,1,0:T(8,128)(2,1)S(1)} async-done(((bf16[8,8,2560]{2,1,0:T(8,128)(2,1)}), bf16[8,8,2560]{2,1,0:T(8,128)(2,1)S(1)}, u32[]{:S(2)}, u32[]{:S(2)}) %all-to-all-start) | async-done | bytes 327712 | tf_op jit(solution)/shard_map/while/body/eval_jaxpr/all_to_all | solution.py:81
  267.9 7.4 %all-to-all-done.1 = bf16[8,8,2560]{2,1,0:T(8,128)(2,1)S(1)} async-done(((bf16[8,8,2560]{2,1,0:T(8,128)(2,1)}), bf16[8,8,2560]{2,1,0:T(8,128)(2,1)S(1)}, u32[]{:S(2)}, u32[]{:S(2)}) %all-to-all-start.1) | async-done | bytes 327712 | tf_op jit(solution)/shard_map/while/body/eval_jaxpr/all_to_all | solution.py:101
  279.4 4.2 collective-permute-done
  289.6 6.7 %all-to-all-done = bf16[8,8,2560]{2,1,0:T(8,128)(2,1)S(1)} async-done(((bf16[8,8,2560]{2,1,0:T(8,128)(2,1)}), bf16[8,8,2560]{2,1,0:T(8,128)(2,1)S(1)}, u32[]{:S(2)}, u32[]{:S(2)}) %all-to-all-start) | async-done | bytes 327712 | tf_op jit(solution)/shard_map/while/body/eval_jaxpr/all_to_all | solution.py:81
  304.3 7.6 %all-to-all-done.1 = bf16[8,8,2560]{2,1,0:T(8,128)(2,1)S(1)} async-done(((bf16[8,8,2560]{2,1,0:T(8,128)(2,1)}), bf16[8,8,2560]{2,1,0:T(8,128)(2,1)S(1)}, u32[]{:S(2)}, u32[]{:S(2)}) %all-to-all-start.1) | async-done | bytes 327712 | tf_op jit(solution)/shard_map/while/body/eval_jaxpr/all_to_all | solution.py:101
  316.1 3.9 collective-permute-done
  325.9 6.7 %all-to-all-done = bf16[8,8,2560]{2,1,0:T(8,128)(2,1)S(1)} async-done(((bf16[8,8,2560]{2,1,0:T(8,128)(2,1)}), bf16[8,8,2560]{2,1,0:T(8,128)(2,1)S(1)}, u32[]{:S(2)}, u32[]{:S(2)}) %all-to-all-start) | async-done | bytes 327712 | tf_op jit(solution)/shard_map/while/body/eval_jaxpr/all_to_all | solution.py:81
  340.7 7.5 %all-to-all-done.1 = bf16[8,8,2560]{2,1,0:T(8,128)(2,1)S(1)} async-done(((bf16[8,8,2560]{2,1,0:T(8,128)(2,1)}), bf16[8,8,2560]{2,1,0:T(8,128)(2,1)S(1)}, u32[]{:S(2)}, u32[]{:S(2)}) %all-to-all-start.1) | async-done | bytes 327712 | tf_op jit(solution)/shard_map/while/body/eval_jaxpr/all_to_all | solution.py:101
  352.4 3.9 collective-permute-done
  358.1 5.6 %all-to-all-start = ((bf16[8,8,2560]{2,1,0:T(8,128)(2,1)}), bf16[8,8,2560]{2,1,0:T(8,128)(2,1)S(1)}, u32[]{:S(2)}, u32[]{:S(2)}) async-start(bf16[8,8,2560]{2,1,0:T(8,128)(2,1)} %bitcast.177), calls=%async_computation | async-start | bytes 655360 | tf_op jit(solution)/shard_map/while/body/eval_jaxpr/all_to_all | solution.py:81
  364.4 6.8 %all-to-all-done = bf16[8,8,2560]{2,1,0:T(8,128)(2,1)S(1)} async-done(((bf16[8,8,2560]{2,1,0:T(8,128)(2,1)}), bf16[8,8,2560]{2,1,0:T(8,128)(2,1)S(1)}, u32[]{:S(2)}, u32[]{:S(2)}) %all-to-all-start) | async-done | bytes 327712 | tf_op jit(solution)/shard_map/while/body/eval_jaxpr/all_to_all | solution.py:81
  379.2 7.4 %all-to-all-done.1 = bf16[8,8,2560]{2,1,0:T(8,128)(2,1)S(1)} async-done(((bf16[8,8,2560]{2,1,0:T(8,128)(2,1)}), bf16[8,8,2560]{2,1,0:T(8,128)(2,1)S(1)}, u32[]{:S(2)}, u32[]{:S(2)}) %all-to-all-start.1) | async-done | bytes 327712 | tf_op jit(solution)/shard_map/while/body/eval_jaxpr/all_to_all | solution.py:101
  390.8 3.9 collective-permute-done
  400.6 7.3 %all-to-all-done = bf16[8,8,2560]{2,1,0:T(8,128)(2,1)S(1)} async-done(((bf16[8,8,2560]{2,1,0:T(8,128)(2,1)}), bf16[8,8,2560]{2,1,0:T(8,128)(2,1)S(1)}, u32[]{:S(2)}, u32[]{:S(2)}) %all-to-all-start) | async-done | bytes 327712 | tf_op jit(solution)/shard_map/while/body/eval_jaxpr/all_to_all | solution.py:81
  412.5 5.4 %all-to-all-start.1 = ((bf16[8,8,2560]{2,1,0:T(8,128)(2,1)}), bf16[8,8,2560]{2,1,0:T(8,128)(2,1)S(1)}, u32[]{:S(2)}, u32[]{:S(2)}) async-start(bf16[8,8,2560]{2,1,0:T(8,128)(2,1)} %fusion.89), calls=%async_computation.1 | async-start | bytes 655360 | tf_op jit(solution)/shard_map/while/body/eval_jaxpr/all_to_all | solution.py:101
  417.9 7.4 %all-to-all-done.1 = bf16[8,8,2560]{2,1,0:T(8,128)(2,1)S(1)} async-done(((bf16[8,8,2560]{2,1,0:T(8,128)(2,1)}), bf16[8,8,2560]{2,1,0:T(8,128)(2,1)S(1)}, u32[]{:S(2)}, u32[]{:S(2)}) %all-to-all-start.1) | async-done | bytes 327712 | tf_op jit(solution)/shard_map/while/body/eval_jaxpr/all_to_all | solution.py:101
  429.5 4.2 collective-permute-done
  433.7 3.9 fusion.32
  439.7 30.6 %reduce-scatter.5.cloned.1.call-done = bf16[1,256,1280]{2,1,0:T(8,128)(2,1)} async-done(((bf16[1,256,2560]{2,1,0:T(8,128)(2,1)}), bf16[1,256,1280]{2,1,0:T(8,128)(2,1)}) %reduce-scatter.5.cloned.1.call-update) | async-done | bytes 655376 | tf_op jit(solution)/shard_map/reduce_scatter | solution.py:154
  470.3 12.8 %reduce-scatter.3.cloned.1.call-done = bf16[1,256,1280]{2,1,0:T(8,128)(2,1)} async-done(((bf16[1,256,2560]{2,1,0:T(8,128)(2,1)}), bf16[1,256,1280]{2,1,0:T(8,128)(2,1)}) %reduce-scatter.3.cloned.1.call-update) | async-done | bytes 655376 | tf_op jit(solution)/shard_map/reduce_scatter | solution.py:151
  (199 shorter events, 138.3 us)
Async XLA Ops:
  7.2 3.1 copy-start.5
  13.8 65.1 %all-to-all-start.2 = ((bf16[1,8,8,8,2560]{4,3,1,0,2:T(8,128)(2,1)}), bf16[1,8,8,8,2560]{4,3,1,0,2:T(8,128)(2,1)}, u32[]{:S(2)}, u32[]{:S(2)}) async-start(bf16[1,8,8,8,2560]{4,3,1,0,2:T(8,128)(2,1)} %bitcast.184), calls=%async_computation.2 | async-start | bytes 5242880 | tf_op jit(solution)/shard_map/all_to_all | solution.py:61
  20.2 2.4 copy-start.3
  20.2 62.2 %all-gather.6.cloned.1.call-start = ((), (), s32[]{:S(2)}) async-start(), calls=%async_computation.6 | async-start | bytes 1966080 | tf_op jit(solution)/shard_map/all_gather | solution.py:43
  20.9 65.2 %all-gather.8.cloned.1.call-start = ((), (), s32[]{:S(2)}) async-start(), calls=%async_computation.7 | async-start | bytes 1966080 | tf_op jit(solution)/shard_map/all_gather | solution.py:42
  21.7 68.4 %all-gather.4.cloned.1.call-start = ((), (), s32[]{:S(2)}) async-start(), calls=%async_computation.5 | async-start | bytes 1966080 | tf_op jit(solution)/shard_map/all_gather | solution.py:44
  22.4 447.9 %reduce-scatter.5.cloned.1.call-start = ((), (), s32[]{:S(2)}) async-start(), calls=%async_computation.9 | async-start | bytes 1966080 | tf_op jit(solution)/shard_map/reduce_scatter | solution.py:154
  86.2 4.7 copy-start
  86.2 4.7 copy-start.4
  86.2 4.7 copy-start.1
  92.7 13.1 %all-to-all-start = ((bf16[8,8,2560]{2,1,0:T(8,128)(2,1)}), bf16[8,8,2560]{2,1,0:T(8,128)(2,1)S(1)}, u32[]{:S(2)}, u32[]{:S(2)}) async-start(bf16[8,8,2560]{2,1,0:T(8,128)(2,1)} %bitcast.177), calls=%async_computation | async-start | bytes 655360 | tf_op jit(solution)/shard_map/while/body/eval_jaxpr/all_to_all | solution.py:81
  110.4 13.5 %all-to-all-start.1 = ((bf16[8,8,2560]{2,1,0:T(8,128)(2,1)}), bf16[8,8,2560]{2,1,0:T(8,128)(2,1)S(1)}, u32[]{:S(2)}, u32[]{:S(2)}) async-start(bf16[8,8,2560]{2,1,0:T(8,128)(2,1)} %fusion.89), calls=%async_computation.1 | async-start | bytes 655360 | tf_op jit(solution)/shard_map/while/body/eval_jaxpr/all_to_all | solution.py:101
  126.7 5.2 %collective-permute-start = (bf16[16,2560]{1,0:T(8,128)(2,1)S(1)}, bf16[16,2560]{1,0:T(8,128)(2,1)S(1)}, u32[]{:S(2)}, u32[]{:S(2)}) collective-permute-start(bf16[16,2560]{1,0:T(8,128)(2,1)S(1)} %fusion.93), channel_id=1, source_target_pairs={{16,0},{17,1},{18,2},{19,3},{20,4},{21,5},{22,6},{23,7},{24,8},{25... | collective-permute-start | bytes 245768 | tf_op jit(solution)/shard_map/while/body/eval_jaxpr/ppermute | solution.py:16
  133.7 12.9 %all-to-all-start = ((bf16[8,8,2560]{2,1,0:T(8,128)(2,1)}), bf16[8,8,2560]{2,1,0:T(8,128)(2,1)S(1)}, u32[]{:S(2)}, u32[]{:S(2)}) async-start(bf16[8,8,2560]{2,1,0:T(8,128)(2,1)} %bitcast.177), calls=%async_computation | async-start | bytes 655360 | tf_op jit(solution)/shard_map/while/body/eval_jaxpr/all_to_all | solution.py:81
  151.2 12.6 %all-to-all-start.1 = ((bf16[8,8,2560]{2,1,0:T(8,128)(2,1)}), bf16[8,8,2560]{2,1,0:T(8,128)(2,1)S(1)}, u32[]{:S(2)}, u32[]{:S(2)}) async-start(bf16[8,8,2560]{2,1,0:T(8,128)(2,1)} %fusion.89), calls=%async_computation.1 | async-start | bytes 655360 | tf_op jit(solution)/shard_map/while/body/eval_jaxpr/all_to_all | solution.py:101
  166.7 5.2 %collective-permute-start = (bf16[16,2560]{1,0:T(8,128)(2,1)S(1)}, bf16[16,2560]{1,0:T(8,128)(2,1)S(1)}, u32[]{:S(2)}, u32[]{:S(2)}) collective-permute-start(bf16[16,2560]{1,0:T(8,128)(2,1)S(1)} %fusion.93), channel_id=1, source_target_pairs={{16,0},{17,1},{18,2},{19,3},{20,4},{21,5},{22,6},{23,7},{24,8},{25... | collective-permute-start | bytes 245768 | tf_op jit(solution)/shard_map/while/body/eval_jaxpr/ppermute | solution.py:16
  173.6 13.1 %all-to-all-start = ((bf16[8,8,2560]{2,1,0:T(8,128)(2,1)}), bf16[8,8,2560]{2,1,0:T(8,128)(2,1)S(1)}, u32[]{:S(2)}, u32[]{:S(2)}) async-start(bf16[8,8,2560]{2,1,0:T(8,128)(2,1)} %bitcast.177), calls=%async_computation | async-start | bytes 655360 | tf_op jit(solution)/shard_map/while/body/eval_jaxpr/all_to_all | solution.py:81
  191.3 11.6 %all-to-all-start.1 = ((bf16[8,8,2560]{2,1,0:T(8,128)(2,1)}), bf16[8,8,2560]{2,1,0:T(8,128)(2,1)S(1)}, u32[]{:S(2)}, u32[]{:S(2)}) async-start(bf16[8,8,2560]{2,1,0:T(8,128)(2,1)} %fusion.89), calls=%async_computation.1 | async-start | bytes 655360 | tf_op jit(solution)/shard_map/while/body/eval_jaxpr/all_to_all | solution.py:101
  205.8 5.2 %collective-permute-start = (bf16[16,2560]{1,0:T(8,128)(2,1)S(1)}, bf16[16,2560]{1,0:T(8,128)(2,1)S(1)}, u32[]{:S(2)}, u32[]{:S(2)}) collective-permute-start(bf16[16,2560]{1,0:T(8,128)(2,1)S(1)} %fusion.93), channel_id=1, source_target_pairs={{16,0},{17,1},{18,2},{19,3},{20,4},{21,5},{22,6},{23,7},{24,8},{25... | collective-permute-start | bytes 245768 | tf_op jit(solution)/shard_map/while/body/eval_jaxpr/ppermute | solution.py:16
  212.8 10.9 %all-to-all-start = ((bf16[8,8,2560]{2,1,0:T(8,128)(2,1)}), bf16[8,8,2560]{2,1,0:T(8,128)(2,1)S(1)}, u32[]{:S(2)}, u32[]{:S(2)}) async-start(bf16[8,8,2560]{2,1,0:T(8,128)(2,1)} %bitcast.177), calls=%async_computation | async-start | bytes 655360 | tf_op jit(solution)/shard_map/while/body/eval_jaxpr/all_to_all | solution.py:81
  228.2 10.9 %all-to-all-start.1 = ((bf16[8,8,2560]{2,1,0:T(8,128)(2,1)}), bf16[8,8,2560]{2,1,0:T(8,128)(2,1)S(1)}, u32[]{:S(2)}, u32[]{:S(2)}) async-start(bf16[8,8,2560]{2,1,0:T(8,128)(2,1)} %fusion.89), calls=%async_computation.1 | async-start | bytes 655360 | tf_op jit(solution)/shard_map/while/body/eval_jaxpr/all_to_all | solution.py:101
  242.0 5.2 %collective-permute-start = (bf16[16,2560]{1,0:T(8,128)(2,1)S(1)}, bf16[16,2560]{1,0:T(8,128)(2,1)S(1)}, u32[]{:S(2)}, u32[]{:S(2)}) collective-permute-start(bf16[16,2560]{1,0:T(8,128)(2,1)S(1)} %fusion.93), channel_id=1, source_target_pairs={{16,0},{17,1},{18,2},{19,3},{20,4},{21,5},{22,6},{23,7},{24,8},{25... | collective-permute-start | bytes 245768 | tf_op jit(solution)/shard_map/while/body/eval_jaxpr/ppermute | solution.py:16
  248.9 10.9 %all-to-all-start = ((bf16[8,8,2560]{2,1,0:T(8,128)(2,1)}), bf16[8,8,2560]{2,1,0:T(8,128)(2,1)S(1)}, u32[]{:S(2)}, u32[]{:S(2)}) async-start(bf16[8,8,2560]{2,1,0:T(8,128)(2,1)} %bitcast.177), calls=%async_computation | async-start | bytes 655360 | tf_op jit(solution)/shard_map/while/body/eval_jaxpr/all_to_all | solution.py:81
  264.4 10.9 %all-to-all-start.1 = ((bf16[8,8,2560]{2,1,0:T(8,128)(2,1)}), bf16[8,8,2560]{2,1,0:T(8,128)(2,1)S(1)}, u32[]{:S(2)}, u32[]{:S(2)}) async-start(bf16[8,8,2560]{2,1,0:T(8,128)(2,1)} %fusion.89), calls=%async_computation.1 | async-start | bytes 655360 | tf_op jit(solution)/shard_map/while/body/eval_jaxpr/all_to_all | solution.py:101
  278.1 5.5 %collective-permute-start = (bf16[16,2560]{1,0:T(8,128)(2,1)S(1)}, bf16[16,2560]{1,0:T(8,128)(2,1)S(1)}, u32[]{:S(2)}, u32[]{:S(2)}) collective-permute-start(bf16[16,2560]{1,0:T(8,128)(2,1)S(1)} %fusion.93), channel_id=1, source_target_pairs={{16,0},{17,1},{18,2},{19,3},{20,4},{21,5},{22,6},{23,7},{24,8},{25... | collective-permute-start | bytes 245768 | tf_op jit(solution)/shard_map/while/body/eval_jaxpr/ppermute | solution.py:16
  285.4 10.9 %all-to-all-start = ((bf16[8,8,2560]{2,1,0:T(8,128)(2,1)}), bf16[8,8,2560]{2,1,0:T(8,128)(2,1)S(1)}, u32[]{:S(2)}, u32[]{:S(2)}) async-start(bf16[8,8,2560]{2,1,0:T(8,128)(2,1)} %bitcast.177), calls=%async_computation | async-start | bytes 655360 | tf_op jit(solution)/shard_map/while/body/eval_jaxpr/all_to_all | solution.py:81
  300.8 11.1 %all-to-all-start.1 = ((bf16[8,8,2560]{2,1,0:T(8,128)(2,1)}), bf16[8,8,2560]{2,1,0:T(8,128)(2,1)S(1)}, u32[]{:S(2)}, u32[]{:S(2)}) async-start(bf16[8,8,2560]{2,1,0:T(8,128)(2,1)} %fusion.89), calls=%async_computation.1 | async-start | bytes 655360 | tf_op jit(solution)/shard_map/while/body/eval_jaxpr/all_to_all | solution.py:101
  314.8 5.2 %collective-permute-start = (bf16[16,2560]{1,0:T(8,128)(2,1)S(1)}, bf16[16,2560]{1,0:T(8,128)(2,1)S(1)}, u32[]{:S(2)}, u32[]{:S(2)}) collective-permute-start(bf16[16,2560]{1,0:T(8,128)(2,1)S(1)} %fusion.93), channel_id=1, source_target_pairs={{16,0},{17,1},{18,2},{19,3},{20,4},{21,5},{22,6},{23,7},{24,8},{25... | collective-permute-start | bytes 245768 | tf_op jit(solution)/shard_map/while/body/eval_jaxpr/ppermute | solution.py:16
  321.8 10.9 %all-to-all-start = ((bf16[8,8,2560]{2,1,0:T(8,128)(2,1)}), bf16[8,8,2560]{2,1,0:T(8,128)(2,1)S(1)}, u32[]{:S(2)}, u32[]{:S(2)}) async-start(bf16[8,8,2560]{2,1,0:T(8,128)(2,1)} %bitcast.177), calls=%async_computation | async-start | bytes 655360 | tf_op jit(solution)/shard_map/while/body/eval_jaxpr/all_to_all | solution.py:81
  337.2 11.0 %all-to-all-start.1 = ((bf16[8,8,2560]{2,1,0:T(8,128)(2,1)}), bf16[8,8,2560]{2,1,0:T(8,128)(2,1)S(1)}, u32[]{:S(2)}, u32[]{:S(2)}) async-start(bf16[8,8,2560]{2,1,0:T(8,128)(2,1)} %fusion.89), calls=%async_computation.1 | async-start | bytes 655360 | tf_op jit(solution)/shard_map/while/body/eval_jaxpr/all_to_all | solution.py:101
  351.1 5.2 %collective-permute-start = (bf16[16,2560]{1,0:T(8,128)(2,1)S(1)}, bf16[16,2560]{1,0:T(8,128)(2,1)S(1)}, u32[]{:S(2)}, u32[]{:S(2)}) collective-permute-start(bf16[16,2560]{1,0:T(8,128)(2,1)S(1)} %fusion.93), channel_id=1, source_target_pairs={{16,0},{17,1},{18,2},{19,3},{20,4},{21,5},{22,6},{23,7},{24,8},{25... | collective-permute-start | bytes 245768 | tf_op jit(solution)/shard_map/while/body/eval_jaxpr/ppermute | solution.py:16
  358.1 13.1 %all-to-all-start = ((bf16[8,8,2560]{2,1,0:T(8,128)(2,1)}), bf16[8,8,2560]{2,1,0:T(8,128)(2,1)S(1)}, u32[]{:S(2)}, u32[]{:S(2)}) async-start(bf16[8,8,2560]{2,1,0:T(8,128)(2,1)} %bitcast.177), calls=%async_computation | async-start | bytes 655360 | tf_op jit(solution)/shard_map/while/body/eval_jaxpr/all_to_all | solution.py:81
  375.7 10.9 %all-to-all-start.1 = ((bf16[8,8,2560]{2,1,0:T(8,128)(2,1)}), bf16[8,8,2560]{2,1,0:T(8,128)(2,1)S(1)}, u32[]{:S(2)}, u32[]{:S(2)}) async-start(bf16[8,8,2560]{2,1,0:T(8,128)(2,1)} %fusion.89), calls=%async_computation.1 | async-start | bytes 655360 | tf_op jit(solution)/shard_map/while/body/eval_jaxpr/all_to_all | solution.py:101
  389.5 5.2 %collective-permute-start = (bf16[16,2560]{1,0:T(8,128)(2,1)S(1)}, bf16[16,2560]{1,0:T(8,128)(2,1)S(1)}, u32[]{:S(2)}, u32[]{:S(2)}) collective-permute-start(bf16[16,2560]{1,0:T(8,128)(2,1)S(1)} %fusion.93), channel_id=1, source_target_pairs={{16,0},{17,1},{18,2},{19,3},{20,4},{21,5},{22,6},{23,7},{24,8},{25... | collective-permute-start | bytes 245768 | tf_op jit(solution)/shard_map/while/body/eval_jaxpr/ppermute | solution.py:16
  396.4 11.5 %all-to-all-start = ((bf16[8,8,2560]{2,1,0:T(8,128)(2,1)}), bf16[8,8,2560]{2,1,0:T(8,128)(2,1)S(1)}, u32[]{:S(2)}, u32[]{:S(2)}) async-start(bf16[8,8,2560]{2,1,0:T(8,128)(2,1)} %bitcast.177), calls=%async_computation | async-start | bytes 655360 | tf_op jit(solution)/shard_map/while/body/eval_jaxpr/all_to_all | solution.py:81
  412.5 12.9 %all-to-all-start.1 = ((bf16[8,8,2560]{2,1,0:T(8,128)(2,1)}), bf16[8,8,2560]{2,1,0:T(8,128)(2,1)S(1)}, u32[]{:S(2)}, u32[]{:S(2)}) async-start(bf16[8,8,2560]{2,1,0:T(8,128)(2,1)} %fusion.89), calls=%async_computation.1 | async-start | bytes 655360 | tf_op jit(solution)/shard_map/while/body/eval_jaxpr/all_to_all | solution.py:101
  428.2 5.5 %collective-permute-start = (bf16[16,2560]{1,0:T(8,128)(2,1)S(1)}, bf16[16,2560]{1,0:T(8,128)(2,1)S(1)}, u32[]{:S(2)}, u32[]{:S(2)}) collective-permute-start(bf16[16,2560]{1,0:T(8,128)(2,1)S(1)} %fusion.93), channel_id=1, source_target_pairs={{16,0},{17,1},{18,2},{19,3},{20,4},{21,5},{22,6},{23,7},{24,8},{25... | collective-permute-start | bytes 245768 | tf_op jit(solution)/shard_map/while/body/eval_jaxpr/ppermute | solution.py:16
  433.7 4.0 copy-start.2
  437.6 45.4 %reduce-scatter.3.cloned.1.call-start = ((), (), s32[]{:S(2)}) async-start(), calls=%async_computation.8 | async-start | bytes 1966080 | tf_op jit(solution)/shard_map/reduce_scatter | solution.py:151
Sparse Core Ops, SparseCore 0:
  22.6 11.4 all-gather.5
  35.6 10.5 all-gather.7
  47.8 10.5 all-gather.3
  437.8 32.4 reduce-scatter.4
  473.0 9.9 reduce-scatter.2
where the time goes:
time: 493 us; the launch traced here: 490 us
  waiting for transfers between devices  257 us (52%)
  starting transfers between devices  93.5 us (19%)
  matrix products  64.2 us (13%)
  other arithmetic  31.9 us (6%)
  local copies, waits for them, and re-layouts  19.4 us (4%)
  between operations  13.9 us (3%)
  blocking collectives  9.03 us (2%)
    all_to_all x9, waiting for transfers between devices, tick_step(): lax.all_to_all(partial_value.reshape(width_all, capacity, feature_count),...  67.7 us
    all_to_all x9, waiting for transfers between devices, tick_step(): lax.all_to_all(sending, 'expert', split_axis=0, concat_axis=0, tiled=True)  62.5 us
    all_to_all x1, waiting for transfers between devices, shards(): lax.all_to_all(unit_send, 'expert', split_axis=2, concat_axis=2, tiled=True)  46 us
    all_to_all x9, starting transfers between devices, tick_step(): lax.all_to_all(sending, 'expert', split_axis=0, concat_axis=0, tiled=True)  38.3 us
    all_to_all x9, starting transfers between devices, tick_step(): lax.all_to_all(partial_value.reshape(width_all, capacity, feature_count),...  37 us
    ppermute x9, waiting for transfers between devices, shifted(): return lax.ppermute(block, axis, route)  35.5 us
    reduce_scatter x1, waiting for transfers between devices, shards(): lax.psum_scatter(part_up.astype(jnp.bfloat16), 'dp', scatter_dimension=2,...  30.6 us
    dot_general x9, matrix products, tick_step(): jnp.einsum('rd,hd->rh', grad_rows, down_slab, preferred_element_type=jnp....  27.9 us
  transfers between devices with their start and end apart: 33, of which 30 were waited for; matrix products, arithmetic and copies ran while one was open for 4% of the time, Pallas kernels for 0%

commit v1 on v0

v1 whole, which is shorter than its diff:
```python
import functools

import jax
import jax.numpy as jnp
from jax import lax
from jax.experimental import pallas as pl
from jax.experimental.pallas import tpu as pltpu
from jax.sharding import PartitionSpec as P

GROUP = 4
EPSILON = 1e-06
F32 = jnp.float32
BF16 = jnp.bfloat16
MESH = pl.DeviceIdType.MESH


def dot(a, b, a_dim, b_dim):
    return lax.dot_general(a, b, (((a_dim,), (b_dim,)), ((), ())), preferred_element_type=F32)


def kernel(
    sizes,
    saved, cot, routes, wg, wu, wd,
    out_gate, out_up,
    weights, head, place, unit_send, unit_full, grad_in, grad_send, grad_full,
    gate_f, up_f, gate_grad, up_grad, part, part_recv, sums, sums_recv, grad_out,
    out_send, out_recv, out_own,
    w_s, w_r, h_s, h_r, u1_s, u1_r, u2_s, u2_r, g1_s, g1_r, g2_s, g2_r,
    a_s, a_r, b_s, b_r, x_s, x_r, o_s, o_r,
):
    sections, experts, n_dp, chunks, rows, tok, width = sizes
    sec = lax.axis_index("pipe")
    here = lax.axis_index("expert")
    core = lax.axis_index("dp")
    e_me = here // GROUP
    q_me = here % GROUP
    last = sections - 1
    half = width // n_dp

    def copy(src, dst, s_sem, r_sem, where):
        return pltpu.make_async_remote_copy(
            src_ref=src, dst_ref=dst, send_sem=s_sem, recv_sem=r_sem,
            device_id=where, device_id_type=MESH)

    def peer(step):
        e = (e_me + step) % experts
        return e, {"expert": e * GROUP + q_me}

    def member(step):
        q = (q_me + step) % GROUP
        return q, {"expert": e_me * GROUP + q}

    def other(step):
        c = (core + step) % n_dp
        return c, {"dp": c}

    barrier = pltpu.get_barrier_semaphore()
    friends = [peer(i)[1] for i in range(1, experts)] + [member(i)[1] for i in range(1, GROUP)]
    friends += [other(i)[1] for i in range(1, n_dp)]
    friends += [{"pipe": (sec + i) % sections} for i in range(1, sections)]
    for friend in friends:
        pl.semaphore_signal(barrier, inc=1, device_id=friend, device_id_type=MESH)
    pl.semaphore_wait(barrier, len(friends))

    def head_copy():
        return copy(cot, head.at[sec], h_s.at[0], h_r.at[sec], {"pipe": sections - 1 + 0 * sec})

    @pl.when(sec != last)
    def _():
        head_copy().start()

    def scale_of(c):
        x = saved[pl.ds(c * tok, tok), :].astype(F32)
        scale = lax.rsqrt(jnp.mean(x * x, axis=1, keepdims=True) + EPSILON)
        return x * scale, scale

    def spread_one(c, rows_b, send, full, s_sem, r_sem):
        ordered = dot(place[c], rows_b, 0, 0).astype(BF16)
        for e in range(experts):
            send[c, e] = ordered[e * rows:(e + 1) * rows]
        for i in range(1, experts):
            e, where = peer(i)
            copy(send.at[c, e], full.at[c, q_me, e_me], s_sem.at[c, e], r_sem.at[c, e_me], where).start()
        full[c, q_me, e_me] = send[c, e_me]

    def spread_two(c, send, full, s1, r1, s2, r2):
        for i in range(1, experts):
            e, where = peer(i)
            copy(send.at[c, e], full.at[c, q_me, e], s1.at[c, e], r1.at[c, e], where).wait_recv()
        for i in range(1, GROUP):
            q, where = member(i)
            copy(full.at[c, q_me], full.at[c, q_me], s2.at[c, q], r2.at[c, q_me], where).start()

    def spread_end(c, full, s2, r2):
        for i in range(1, GROUP):
            q, where = member(i)
            copy(full.at[c, q_me], full.at[c, q], s2.at[c, q], r2.at[c, q], where).wait_recv()

    for c in range(chunks):
        chosen = routes[pl.ds(c * tok, tok), :]
        lanes = max(128, experts)
        onehot = (chosen == lax.broadcasted_iota(jnp.int32, (tok, lanes), 1)).astype(F32)
        below = (lax.broadcasted_iota(jnp.int32, (tok, tok), 1)
                 < lax.broadcasted_iota(jnp.int32, (tok, tok), 0)).astype(F32)
        ahead = dot(below.astype(BF16), onehot.astype(BF16), 1, 0)
        rank = jnp.sum(ahead * onehot, axis=1, keepdims=True)
        slot = chosen * rows + rank.astype(jnp.int32)
        place[c] = (slot == lax.broadcasted_iota(jnp.int32, (tok, tok), 1)).astype(F32).astype(BF16)
        unit, _ = scale_of(c)
        spread_one(c, unit.astype(BF16), unit_send, unit_full, u1_s, u1_r)

    for k, ref in enumerate((wg, wu, wd)):
        for i in range(1, n_dp):
            d, where = other(i)
            copy(ref, weights.at[k, core], w_s.at[k, d], w_r.at[k, core], where).start()
        weights[k, core] = ref[...]

    @pl.when(sec == last)
    def _():
        cols = width // sections
        for s in range(last):
            copy(cot, head.at[s], h_s.at[0], h_r.at[s], {"pipe": s}).wait_recv()
        for c in range(chunks):
            for s in range(sections):
                source = cot if s == last else head.at[s]
                grad_in[c, :, s * cols:(s + 1) * cols] = source[c * tok:(c + 1) * tok, :]
            spread_one(c, grad_in[c], grad_send, grad_full, g1_s, g1_r)

    for c in range(chunks):
        spread_two(c, unit_send, unit_full, u1_s, u1_r, u2_s, u2_r)

    @pl.when(sec == last)
    def _():
        for c in range(chunks):
            spread_two(c, grad_send, grad_full, g1_s, g1_r, g2_s, g2_r)

    for k, ref in enumerate((wg, wu, wd)):
        for i in range(1, n_dp):
            d, where = other(i)
            copy(ref, weights.at[k, d], w_s.at[k, d], w_r.at[k, d], where).wait_recv()

    per_block = GROUP if GROUP * experts * rows <= 256 else 1
    blocks = [(first, per_block) for first in range(0, GROUP, per_block)]
    block_rows = per_block * experts * rows

    def rows_of(full, c, first, count):
        return full[c, first:first + count].reshape(block_rows, width)

    def project(x, k):
        total = dot(x[:, :half], weights[k, 0], 1, 1)
        for d in range(1, n_dp):
            total = total + dot(x[:, d * half:(d + 1) * half], weights[k, d], 1, 1)
        return total

    for c in range(chunks):
        spread_end(c, unit_full, u2_s, u2_r)
        for first, count in blocks:
            x = rows_of(unit_full, c, first, count)
            at = pl.ds(c * GROUP * experts * rows + first * experts * rows, block_rows)
            gate_f[at, :] = project(x, 0)
            up_f[at, :] = project(x, 1)

    def backward(c):
        spread_end(c, grad_full, g2_s, g2_r)
        for first, count in blocks:
            at = pl.ds(c * GROUP * experts * rows + first * experts * rows, block_rows)
            hidden_grad = project(rows_of(grad_full, c, first, count), 2)
            gate = gate_f[at, :]
            up = up_f[at, :]
            sig = jax.nn.sigmoid(gate)
            gate_g = (hidden_grad * up * sig * (1.0 + gate * (1.0 - sig))).astype(BF16)
            up_g = (hidden_grad * gate * sig).astype(BF16)
            gate_grad[at, :] = gate_g
            up_grad[at, :] = up_g

            @pl.when(sec > 0)
            def _():
                for d in range(n_dp):
                    value = dot(gate_g, weights[0, d], 1, 0) + dot(up_g, weights[1, d], 1, 0)
                    part[c, first:first + count, :, :, d * half:(d + 1) * half] = (
                        value.astype(BF16).reshape(count, experts, rows, half))

        @pl.when(sec > 0)
        def _():
            for i in range(1, GROUP):
                q, where = member(i)
                copy(part.at[c, q], part_recv.at[c, q_me], a_s.at[c, q], a_r.at[c, q_me], where).start()

    def fold(c):
        total = part[c, q_me].astype(F32)
        for i in range(1, GROUP):
            q, where = member(i)
            copy(part.at[c, q], part_recv.at[c, q], a_s.at[c, q], a_r.at[c, q], where).wait_recv()
            total = total + part_recv[c, q].astype(F32)
        sums[c] = total.astype(BF16)
        for i in range(1, experts):
            e, where = peer(i)
            copy(sums.at[c, e], sums_recv.at[c, e_me], b_s.at[c, e], b_r.at[c, e_me], where).start()
        sums_recv[c, e_me] = sums[c, e_me]

    def x_copy(c):
        return copy(grad_out.at[c], grad_in.at[c], x_s.at[c], x_r.at[c],
                    {"pipe": (sec + sections - 1) % sections})

    def finish(c):
        for i in range(1, experts):
            e, where = peer(i)
            copy(sums.at[c, e], sums_recv.at[c, e], b_s.at[c, e], b_r.at[c, e], where).wait_recv()
        unit_g = dot(place[c], sums_recv[c].reshape(tok, width), 1, 0)
        unit, scale = scale_of(c)
        norm = scale * (unit_g - unit * jnp.mean(unit_g * unit, axis=1, keepdims=True))
        grad_out[c] = (grad_in[c].astype(F32) + norm).astype(BF16)
        x_copy(c).start()

    for t in range(chunks + 2):
        if t < chunks:
            @pl.when(sec != last)
            def _():
                x_copy(t).wait_recv()
                spread_one(t, grad_in[t], grad_send, grad_full, g1_s, g1_r)
                spread_two(t, grad_send, grad_full, g1_s, g1_r, g2_s, g2_r)

            backward(t)

        @pl.when(sec > 0)
        def _():
            if 0 <= t - 1 < chunks:
                fold(t - 1)
            if 0 <= t - 2 < chunks:
                finish(t - 2)

    all_rows = chunks * GROUP * experts * rows

    def o_copy(k, i, mine):
        d, where = other(i)
        return copy(out_send.at[k, d], out_recv.at[k, core if mine else d],
                    o_s.at[k, d], o_r.at[k, core if mine else d], where)

    for k, ref in enumerate((gate_grad, up_grad)):
        left = ref[...]
        for d in range(n_dp):
            right = unit_full[:, :, :, :, d * half:(d + 1) * half].reshape(all_rows, half)
            out_send[k, d] = dot(left, right, 0, 0).astype(BF16)
        for i in range(1, n_dp):
            o_copy(k, i, True).start()
    for k, out in enumerate((out_gate, out_up)):
        total = out_send[k, core].astype(F32)
        for i in range(1, n_dp):
            d, _ = other(i)
            o_copy(k, i, False).wait_recv()
            total = total + out_recv[k, d].astype(F32)
        out[...] = total.astype(BF16)

    for k, ref in enumerate((wg, wu, wd)):
        for i in range(1, n_dp):
            d, where = other(i)
            copy(ref, weights.at[k, d], w_s.at[k, d], w_r.at[k, d], where).wait_send()
    for k in range(2):
        for i in range(1, n_dp):
            o_copy(k, i, True).wait_send()

    @pl.when(sec != last)
    def _():
        head_copy().wait_send()

    for c in range(chunks):
        for i in range(1, experts):
            e, where = peer(i)
            copy(unit_send.at[c, e], unit_full.at[c, q_me, e], u1_s.at[c, e], u1_r.at[c, e], where).wait_send()
            copy(grad_send.at[c, e], grad_full.at[c, q_me, e], g1_s.at[c, e], g1_r.at[c, e], where).wait_send()
        for i in range(1, GROUP):
            q, where = member(i)
            copy(unit_full.at[c, q_me], unit_full.at[c, q], u2_s.at[c, q], u2_r.at[c, q], where).wait_send()
            copy(grad_full.at[c, q_me], grad_full.at[c, q], g2_s.at[c, q], g2_r.at[c, q], where).wait_send()

    @pl.when(sec > 0)
    def _():
        for c in range(chunks):
            for i in range(1, GROUP):
                q, where = member(i)
                copy(part.at[c, q], part_recv.at[c, q], a_s.at[c, q], a_r.at[c, q], where).wait_send()
            for i in range(1, experts):
                e, where = peer(i)
                copy(sums.at[c, e], sums_recv.at[c, e], b_s.at[c, e], b_r.at[c, e], where).wait_send()
            x_copy(c).wait_send()


def shards(mesh, saved, cotangent, routes, w_gate, w_up, w_down):
    sections, spots, n_dp = mesh.shape["pipe"], mesh.shape["expert"], mesh.shape["dp"]
    experts = spots // GROUP
    tokens, width = saved.shape[2], saved.shape[3]
    hidden, half = w_gate.shape[2], w_gate.shape[3]
    chunks = max(1, min(4, tokens // (experts * 16)))
    tok = tokens // chunks
    rows = tok // experts
    sizes = (sections, experts, n_dp, chunks, rows, tok, width)
    all_rows = chunks * GROUP * experts * rows
    full = (chunks, GROUP, experts, rows, width)
    own = (chunks, experts, rows, width)
    dma = pltpu.SemaphoreType.DMA
    vm = pltpu.VMEM
    result = jax.ShapeDtypeStruct((hidden, half), BF16)
    scratch = [
        vm((3, n_dp, hidden, half), BF16),
        vm((sections,) + cotangent.shape, BF16),
        vm((chunks, tok, tok), BF16),
        vm(own, BF16), vm(full, BF16),
        vm((chunks, tok, width), BF16),
        vm(own, BF16), vm(full, BF16),
        vm((all_rows, hidden), F32), vm((all_rows, hidden), F32),
        vm((all_rows, hidden), BF16), vm((all_rows, hidden), BF16),
        vm(full, BF16), vm(full, BF16),
        vm(own, BF16), vm(own, BF16),
        vm((chunks, tok, width), BF16),
        vm((2, n_dp, hidden, half), BF16), vm((2, n_dp, hidden, half), BF16),
        vm((8, 128), F32),
        dma((3, n_dp)), dma((3, n_dp)),
        dma((1,)), dma((sections,)),
        dma((chunks, experts)), dma((chunks, experts)),
        dma((chunks, GROUP)), dma((chunks, GROUP)),
        dma((chunks, experts)), dma((chunks, experts)),
        dma((chunks, GROUP)), dma((chunks, GROUP)),
        dma((chunks, GROUP)), dma((chunks, GROUP)),
        dma((chunks, experts)), dma((chunks, experts)),
        dma((chunks,)), dma((chunks,)),
        dma((2, n_dp)), dma((2, n_dp)),
    ]
    flops = 14 * all_rows * hidden * width
    gate, up = pl.pallas_call(
        functools.partial(kernel, sizes),
        out_shape=(result, result),
        in_specs=[pl.BlockSpec(memory_space=pltpu.VMEM)] * 6,
        out_specs=[pl.BlockSpec(memory_space=pltpu.VMEM)] * 2,
        scratch_shapes=scratch,
        compiler_params=pltpu.CompilerParams(
            collective_id=0, has_side_effects=True, vmem_limit_bytes=52 * 1024 * 1024),
        cost_estimate=pl.CostEstimate(
            flops=flops, bytes_accessed=12 * hidden * half, transcendentals=all_rows * hidden),
    )(saved[0, 0], cotangent, routes[0, 0], w_gate[0, 0], w_up[0, 0], w_down[0, 0])
    return gate[None, None], up[None, None]


def solution(mesh):
    weight = P(None, "pipe", "expert", "dp")
    rows = P(None, "pipe", ("expert", "dp"), None)
    in_specs = (rows, P(("expert", "dp"), "pipe"), rows, weight, weight, weight)
    return jax.shard_map(
        functools.partial(shards, mesh), mesh=mesh, in_specs=in_specs,
        out_specs=(weight, weight), check_vma=False)
```

time: 493 us -> 171 us (0.35)
  waiting for transfers between devices: 257 us -> 0 us
  Pallas kernels: 0 us -> 166 us
  starting transfers between devices: 93.5 us -> 0 us
  matrix products: 64.2 us -> 0 us
  other arithmetic: 31.9 us -> 0 us
  local copies, waits for them, and re-layouts: 19.4 us -> 3.4 us
  between operations: 13.9 us -> 0.65 us
  blocking collectives: 9.03 us -> 0 us
    all_to_all x19 -> x0, waiting for transfers between devices: 176 us -> none  [the longest x9 67.7 us: tick_step(): lax.all_to_all(partial_value.reshape(width_all, capacity, feature_count),...]
    pallas_call x0 -> x1, Pallas kernels: none -> 166 us  [shards(): pl.pallas_call(functools.partial(kernel, sizes), out_shape=(result, resul...]
    all_to_all x19 -> x0, starting transfers between devices: 81.7 us -> none  [the longest x9 38.3 us: tick_step(): lax.all_to_all(sending, 'expert', split_axis=0, concat_axis=0, tiled=True)]
    dot_general x41 -> x0, matrix products: 64.2 us -> none  [the longest x9 27.9 us: tick_step(): jnp.einsum('rd,hd->rh', grad_rows, down_slab, preferred_element_type=jnp....]
    reduce_scatter x2 -> x0, waiting for transfers between devices: 43.4 us -> none  [the longest x1 30.6 us: shards(): lax.psum_scatter(part_up.astype(jnp.bfloat16), 'dp', scatter_dimension=2,...]
    ppermute x9 -> x0, waiting for transfers between devices: 35.5 us -> none  [shifted(): return lax.ppermute(block, axis, route)]
    reduce_sum x19 -> x0, other arithmetic: 11.8 us -> none  [the longest x9 10.1 us: tick_step(): jnp.mean(unit_grad * unit_here, axis=1, keepdims=True)]
    ppermute x9 -> x0, starting transfers between devices: 11.6 us -> none  [shifted(): return lax.ppermute(block, axis, route)]
  transfers between devices with their start and end apart: 33 -> 0, of which waited for: 30 -> 0; matrix products, arithmetic and copies ran while one was open for 4% -> 0% of each run, Pallas kernels for 0% -> 0%
where the time goes in v1:
time: 171 us; the launch traced here: 170 us
  Pallas kernels  166 us (97%)
  local copies, waits for them, and re-layouts  3.4 us (2%)
    pallas_call x1, Pallas kernels, shards(): pl.pallas_call(functools.partial(kernel, sizes), out_shape=(result, resul...  166 us

profile of v1, /device:TPU:1, one launch (start us, length us, event | category | flops | bytes accessed | tf_op | source)
XLA Modules:
  0.0 169.7 jit_solution(6123825634233537567)
XLA Ops:
  0.6 0.0 copy-start.1
  0.6 0.6 copy-done.1
  1.3 0.1 copy.8.routes
  1.4 0.0 copy-start
  1.4 1.0 copy-done
  2.4 165.6 %shard_map.77 = (bf16[256,1280]{1,0:T(8,128)(2,1)S(1)}, bf16[256,1280]{1,0:T(8,128)(2,1)S(1)}) custom-call(bf16[128,2560]{1,0:T(8,128)(2,1)} %bitcast.10, bf16[128,1280]{1,0:T(8,128)(2,1)S(1)} %copy-done, s32[128,1]{1,0:T(8,128)S(1)} %copy.8.routes, bf16[256,1280]{1,0:T(8,128)(2,1)} %bitcast.11, bf16[256,1280]{1,0:T(8,128)(2,1)} %bitcast.12, ...), custom_call_target="tpu_custom_call" | custom-call | flops 4697620480 | bytes 3932160 | tf_op jit(solution)/shard_map/pallas_call | solution.py:329
  168.0 0.8 copy.11
  168.8 0.8 copy.12
Async XLA Ops:
  0.6 0.7 copy-start.1
  1.4 1.0 copy-start

commit v2 on v1

--- a/solution.py
+++ b/solution.py
@@ -23,8 +23,8 @@
     saved, cot, routes, wg, wu, wd,
     out_gate, out_up,
     weights, head, place, unit_send, unit_full, grad_in, grad_send, grad_full,
-    gate_f, up_f, gate_grad, up_grad, part, part_recv, sums, sums_recv, grad_out,
-    out_send, out_recv, out_own,
+    gate_f, up_f, gate_grad, up_grad, part, part_recv, middle, sums, sums_recv, grad_out,
+    out_send, out_recv, early,
     w_s, w_r, h_s, h_r, u1_s, u1_r, u2_s, u2_r, g1_s, g1_r, g2_s, g2_r,
     a_s, a_r, b_s, b_r, x_s, x_r, o_s, o_r,
 ):
@@ -46,16 +46,20 @@
         e = (e_me + step) % experts
         return e, {"expert": e * GROUP + q_me}
 
-    def member(step):
-        q = (q_me + step) % GROUP
-        return q, {"expert": e_me * GROUP + q}
+    q_y = q_me + 1 - 2 * (q_me % 2)
+    q_z = (q_me + 2) % GROUP
+    q_far = GROUP - 1 - q_me
+    to_y = {"expert": e_me * GROUP + q_y}
+    to_z = {"expert": e_me * GROUP + q_z}
+    cut = max(128, width * 3 // 4 // 128 * 128)
+    major, minor = pl.ds(0, cut), pl.ds(cut, width - cut)
 
     def other(step):
         c = (core + step) % n_dp
         return c, {"dp": c}
 
     barrier = pltpu.get_barrier_semaphore()
-    friends = [peer(i)[1] for i in range(1, experts)] + [member(i)[1] for i in range(1, GROUP)]
+    friends = [peer(i)[1] for i in range(1, experts)] + [to_y, to_z]
     friends += [other(i)[1] for i in range(1, n_dp)]
     friends += [{"pipe": (sec + i) % sections} for i in range(1, sections)]
     for friend in friends:
@@ -87,14 +91,24 @@
         for i in range(1, experts):
             e, where = peer(i)
             copy(send.at[c, e], full.at[c, q_me, e], s1.at[c, e], r1.at[c, e], where).wait_recv()
-        for i in range(1, GROUP):
-            q, where = member(i)
-            copy(full.at[c, q_me], full.at[c, q_me], s2.at[c, q], r2.at[c, q_me], where).start()
+        group_copy(c, full, s2, r2, 0, q_me).start()
+        group_copy(c, full, s2, r2, 1, q_me).start()
+
+    def group_copy(c, full, s2, r2, kind, q):
+        ref = full.at[c, q]
+        if kind >= 2:
+            ref = ref.at[:, :, major if kind == 2 else minor]
+        return copy(ref, ref, s2.at[c, kind], r2.at[c, kind], to_z if kind % 2 else to_y)
+
+    def relay(c, full, s2, r2):
+        group_copy(c, full, s2, r2, 1, q_z).wait_recv()
+        group_copy(c, full, s2, r2, 2, q_z).start()
+        group_copy(c, full, s2, r2, 0, q_y).wait_recv()
+        group_copy(c, full, s2, r2, 3, q_y).start()
 
     def spread_end(c, full, s2, r2):
-        for i in range(1, GROUP):
-            q, where = member(i)
-            copy(full.at[c, q_me], full.at[c, q], s2.at[c, q], r2.at[c, q], where).wait_recv()
+        group_copy(c, full, s2, r2, 2, q_far).wait_recv()
+        group_copy(c, full, s2, r2, 3, q_far).wait_recv()
 
     for c in range(chunks):
         chosen = routes[pl.ds(c * tok, tok), :]
@@ -129,9 +143,11 @@
     for c in range(chunks):
         spread_two(c, unit_send, unit_full, u1_s, u1_r, u2_s, u2_r)
 
-    @pl.when(sec == last)
-    def _():
-        for c in range(chunks):
+    for c in range(chunks):
+        relay(c, unit_full, u2_s, u2_r)
+
+        @pl.when(sec == last)
+        def _():
             spread_two(c, grad_send, grad_full, g1_s, g1_r, g2_s, g2_r)
 
     for k, ref in enumerate((wg, wu, wd)):
@@ -182,16 +198,31 @@
 
         @pl.when(sec > 0)
         def _():
-            for i in range(1, GROUP):
-                q, where = member(i)
-                copy(part.at[c, q], part_recv.at[c, q_me], a_s.at[c, q], a_r.at[c, q_me], where).start()
+            for kind in (1, 3, 0, 2):
+                back_copy(c, kind).start()
+
+    def back_copy(c, kind):
+        cols = major if kind in (0, 1, 4) else minor
+        if kind < 4:
+            q = (q_y, q_far, q_z, q_far)[kind]
+            src, slot, where = part.at[c, q], kind % 2, (to_y if kind < 2 else to_z)
+        else:
+            src, slot, where = middle.at[c], 2, (to_z if kind == 4 else to_y)
+        return copy(src.at[:, :, cols], part_recv.at[c, slot].at[:, :, cols],
+                    a_s.at[c, kind], a_r.at[c, kind], where)
+
+    def pair(c):
+        for kind, cols, q in ((1, slice(0, cut), q_z), (3, slice(cut, width), q_y)):
+            back_copy(c, kind).wait_recv()
+            middle[c, :, :, cols] = (
+                part[c, q, :, :, cols].astype(F32) + part_recv[c, 1, :, :, cols].astype(F32)
+            ).astype(BF16)
+            back_copy(c, 4 if kind == 1 else 5).start()
 
     def fold(c):
-        total = part[c, q_me].astype(F32)
-        for i in range(1, GROUP):
-            q, where = member(i)
-            copy(part.at[c, q], part_recv.at[c, q], a_s.at[c, q], a_r.at[c, q], where).wait_recv()
-            total = total + part_recv[c, q].astype(F32)
+        for kind in (0, 2, 4, 5):
+            back_copy(c, kind).wait_recv()
+        total = part[c, q_me].astype(F32) + part_recv[c, 0].astype(F32) + part_recv[c, 2].astype(F32)
         sums[c] = total.astype(BF16)
         for i in range(1, experts):
             e, where = peer(i)
@@ -212,35 +243,64 @@
         grad_out[c] = (grad_in[c].astype(F32) + norm).astype(BF16)
         x_copy(c).start()
 
-    for t in range(chunks + 2):
+    chunk_rows = GROUP * experts * rows
+
+    def outer(k, d, first, count):
+        left = (gate_grad, up_grad)[k][pl.ds(first * chunk_rows, count * chunk_rows), :]
+        right = unit_full[first:first + count, :, :, :, d * half:(d + 1) * half]
+        return dot(left, right.reshape(count * chunk_rows, half), 0, 0)
+
+    def sum_early():
+        for k in range(2):
+            for d in range(n_dp):
+                early[k, d] = outer(k, d, 0, chunks - 1)
+
+    @pl.when(sec == last)
+    def _():
+        relay(0, grad_full, g2_s, g2_r)
+
+    for t in range(chunks + 3):
         if t < chunks:
+            if t > 0 and t == chunks - 1:
+                pl.when(sec == 0)(sum_early)
+
+            if t + 1 < chunks:
+                @pl.when(sec == last)
+                def _():
+                    relay(t + 1, grad_full, g2_s, g2_r)
+
             @pl.when(sec != last)
             def _():
                 x_copy(t).wait_recv()
                 spread_one(t, grad_in[t], grad_send, grad_full, g1_s, g1_r)
                 spread_two(t, grad_send, grad_full, g1_s, g1_r, g2_s, g2_r)
+                relay(t, grad_full, g2_s, g2_r)
 
             backward(t)
 
         @pl.when(sec > 0)
         def _():
             if 0 <= t - 1 < chunks:
-                fold(t - 1)
+                pair(t - 1)
             if 0 <= t - 2 < chunks:
-                finish(t - 2)
-
-    all_rows = chunks * GROUP * experts * rows
+                fold(t - 2)
+            if 0 <= t - 3 < chunks:
+                finish(t - 3)
+
+    if chunks > 1:
+        pl.when(sec > 0)(sum_early)
 
     def o_copy(k, i, mine):
         d, where = other(i)
         return copy(out_send.at[k, d], out_recv.at[k, core if mine else d],
                     o_s.at[k, d], o_r.at[k, core if mine else d], where)
 
-    for k, ref in enumerate((gate_grad, up_grad)):
-        left = ref[...]
+    for k in range(2):
         for d in range(n_dp):
-            right = unit_full[:, :, :, :, d * half:(d + 1) * half].reshape(all_rows, half)
-            out_send[k, d] = dot(left, right, 0, 0).astype(BF16)
+            value = outer(k, d, chunks - 1, 1)
+            if chunks > 1:
+                value = value + early[k, d]
+            out_send[k, d] = value.astype(BF16)
         for i in range(1, n_dp):
             o_copy(k, i, True).start()
     for k, out in enumerate((out_gate, out_up)):
@@ -268,17 +328,15 @@
             e, where = peer(i)
             copy(unit_send.at[c, e], unit_full.at[c, q_me, e], u1_s.at[c, e], u1_r.at[c, e], where).wait_send()
             copy(grad_send.at[c, e], grad_full.at[c, q_me, e], g1_s.at[c, e], g1_r.at[c, e], where).wait_send()
-        for i in range(1, GROUP):
-            q, where = member(i)
-            copy(unit_full.at[c, q_me], unit_full.at[c, q], u2_s.at[c, q], u2_r.at[c, q], where).wait_send()
-            copy(grad_full.at[c, q_me], grad_full.at[c, q], g2_s.at[c, q], g2_r.at[c, q], where).wait_send()
+        for kind, q in enumerate((q_me, q_me, q_z, q_y)):
+            group_copy(c, unit_full, u2_s, u2_r, kind, q).wait_send()
+            group_copy(c, grad_full, g2_s, g2_r, kind, q).wait_send()
 
     @pl.when(sec > 0)
     def _():
         for c in range(chunks):
-            for i in range(1, GROUP):
-                q, where = member(i)
-                copy(part.at[c, q], part_recv.at[c, q], a_s.at[c, q], a_r.at[c, q], where).wait_send()
+            for kind in range(6):
+                back_copy(c, kind).wait_send()
             for i in range(1, experts):
                 e, where = peer(i)
                 copy(sums.at[c, e], sums_recv.at[c, e], b_s.at[c, e], b_r.at[c, e], where).wait_send()
@@ -309,18 +367,18 @@
         vm(own, BF16), vm(full, BF16),
         vm((all_rows, hidden), F32), vm((all_rows, hidden), F32),
         vm((all_rows, hidden), BF16), vm((all_rows, hidden), BF16),
-        vm(full, BF16), vm(full, BF16),
+        vm(full, BF16), vm((chunks, 3) + own[1:], BF16), vm(own, BF16),
         vm(own, BF16), vm(own, BF16),
         vm((chunks, tok, width), BF16),
         vm((2, n_dp, hidden, half), BF16), vm((2, n_dp, hidden, half), BF16),
-        vm((8, 128), F32),
+        vm((2, n_dp, hidden, half), F32),
         dma((3, n_dp)), dma((3, n_dp)),
         dma((1,)), dma((sections,)),
         dma((chunks, experts)), dma((chunks, experts)),
         dma((chunks, GROUP)), dma((chunks, GROUP)),
         dma((chunks, experts)), dma((chunks, experts)),
         dma((chunks, GROUP)), dma((chunks, GROUP)),
-        dma((chunks, GROUP)), dma((chunks, GROUP)),
+        dma((chunks, 6)), dma((chunks, 6)),
         dma((chunks, experts)), dma((chunks, experts)),
         dma((chunks,)), dma((chunks,)),
         dma((2, n_dp)), dma((2, n_dp)),

time: 171 us -> 166 us (0.971)
  Pallas kernels: 166 us -> 162 us
    pallas_call x1, Pallas kernels: 166 us -> 162 us  [shards(): pl.pallas_call(functools.partial(kernel, sizes), out_shape=(result, resul...]
where the time goes in v2:
time: 166 us
  Pallas kernels  162 us (98%)
  local copies, waits for them, and re-layouts  3.4 us (2%)
    pallas_call x1, Pallas kernels, shards(): pl.pallas_call(functools.partial(kernel, sizes), out_shape=(result, resul...  162 us

profile of v2, /device:TPU:1, one launch (start us, length us, event | category | flops | bytes accessed | tf_op | source)
XLA Modules:
  0.0 166.1 jit_solution(13436755293070612834)
XLA Ops:
  0.6 0.0 copy-start.1
  0.6 0.6 copy-done.1
  1.3 0.1 copy.8.routes
  1.4 0.0 copy-start
  1.4 1.0 copy-done
  2.4 162.1 %shard_map.77 = (bf16[256,1280]{1,0:T(8,128)(2,1)S(1)}, bf16[256,1280]{1,0:T(8,128)(2,1)S(1)}) custom-call(bf16[128,2560]{1,0:T(8,128)(2,1)} %bitcast.10, bf16[128,1280]{1,0:T(8,128)(2,1)S(1)} %copy-done, s32[128,1]{1,0:T(8,128)S(1)} %copy.8.routes, bf16[256,1280]{1,0:T(8,128)(2,1)} %bitcast.11, bf16[256,1280]{1,0:T(8,128)(2,1)} %bitcast.12, ...), custom_call_target="tpu_custom_call" | custom-call | flops 4697620480 | bytes 3932160 | tf_op jit(solution)/shard_map/pallas_call | solution.py:387
  164.5 0.8 copy.11
  165.3 0.8 copy.12
Async XLA Ops:
  0.6 0.7 copy-start.1
  1.4 1.0 copy-start

commit v3 on v2

--- a/solution.py
+++ b/solution.py
@@ -247,7 +247,7 @@
 
     def outer(k, d, first, count):
         left = (gate_grad, up_grad)[k][pl.ds(first * chunk_rows, count * chunk_rows), :]
-        right = unit_full[first:first + count, :, :, :, d * half:(d + 1) * half]
+        right = unit_full[first:first + count, :, :, :, pl.ds(pl.multiple_of(d * half, 128), half)]
         return dot(left, right.reshape(count * chunk_rows, half), 0, 0)
 
     def sum_early():
@@ -255,27 +255,20 @@
             for d in range(n_dp):
                 early[k, d] = outer(k, d, 0, chunks - 1)
 
-    @pl.when(sec == last)
-    def _():
-        relay(0, grad_full, g2_s, g2_r)
-
-    for t in range(chunks + 3):
-        if t < chunks:
+    for t in range(-3, chunks + 3):
+        @pl.when(sec != last)
+        def _():
+            if 0 <= t + 3 < chunks:
+                x_copy(t + 3).wait_recv()
+                spread_one(t + 3, grad_in[t + 3], grad_send, grad_full, g1_s, g1_r)
+            if 0 <= t + 2 < chunks:
+                spread_two(t + 2, grad_send, grad_full, g1_s, g1_r, g2_s, g2_r)
+
+        if 0 <= t + 1 < chunks:
+            relay(t + 1, grad_full, g2_s, g2_r)
+        if 0 <= t < chunks:
             if t > 0 and t == chunks - 1:
                 pl.when(sec == 0)(sum_early)
-
-            if t + 1 < chunks:
-                @pl.when(sec == last)
-                def _():
-                    relay(t + 1, grad_full, g2_s, g2_r)
-
-            @pl.when(sec != last)
-            def _():
-                x_copy(t).wait_recv()
-                spread_one(t, grad_in[t], grad_send, grad_full, g1_s, g1_r)
-                spread_two(t, grad_send, grad_full, g1_s, g1_r, g2_s, g2_r)
-                relay(t, grad_full, g2_s, g2_r)
-
             backward(t)
 
         @pl.when(sec > 0)
@@ -295,14 +288,18 @@
         return copy(out_send.at[k, d], out_recv.at[k, core if mine else d],
                     o_s.at[k, d], o_r.at[k, core if mine else d], where)
 
+    def outer_all(k, d):
+        value = outer(k, d, chunks - 1, 1)
+        if chunks > 1:
+            value = value + early[k, d]
+        out_send[k, d] = value.astype(BF16)
+
     for k in range(2):
-        for d in range(n_dp):
-            value = outer(k, d, chunks - 1, 1)
-            if chunks > 1:
-                value = value + early[k, d]
-            out_send[k, d] = value.astype(BF16)
-        for i in range(1, n_dp):
+        for i in range(1, n_dp):
+            outer_all(k, other(i)[0])
             o_copy(k, i, True).start()
+    for k in range(2):
+        outer_all(k, core)
     for k, out in enumerate((out_gate, out_up)):
         total = out_send[k, core].astype(F32)
         for i in range(1, n_dp):

time: 166 us -> 141 us (0.85)
  Pallas kernels: 162 us -> 137 us
    pallas_call x1, Pallas kernels: 162 us -> 137 us  [shards(): pl.pallas_call(functools.partial(kernel, sizes), out_shape=(result, resul...]
where the time goes in v3:
time: 141 us
  Pallas kernels  137 us (97%)
  local copies, waits for them, and re-layouts  3.4 us (2%)
    pallas_call x1, Pallas kernels, shards(): pl.pallas_call(functools.partial(kernel, sizes), out_shape=(result, resul...  137 us
    unnamed x6, local copies, waits for them, and re-layouts  3.29 us

profile of v3, /device:TPU:1, one launch (start us, length us, event | category | flops | bytes accessed | tf_op | source)
XLA Modules:
  0.0 140.9 jit_solution(4305182646761620733)
XLA Ops:
  0.6 0.0 copy-start.1
  0.6 0.6 copy-done.1
  1.3 0.1 copy.8.routes
  1.4 0.0 copy-start
  1.4 1.0 copy-done
  2.4 136.8 %shard_map.77 = (bf16[256,1280]{1,0:T(8,128)(2,1)S(1)}, bf16[256,1280]{1,0:T(8,128)(2,1)S(1)}) custom-call(bf16[128,2560]{1,0:T(8,128)(2,1)} %bitcast.10, bf16[128,1280]{1,0:T(8,128)(2,1)S(1)} %copy-done, s32[128,1]{1,0:T(8,128)S(1)} %copy.8.routes, bf16[256,1280]{1,0:T(8,128)(2,1)} %bitcast.11, bf16[256,1280]{1,0:T(8,128)(2,1)} %bitcast.12, ...), custom_call_target="tpu_custom_call" | custom-call | flops 4697620480 | bytes 3932160 | tf_op jit(solution)/shard_map/pallas_call | solution.py:384
  139.2 0.8 copy.11
  140.0 0.8 copy.12
Async XLA Ops:
  0.6 0.7 copy-start.1
  1.4 1.0 copy-start

commit v4 on v3

--- a/solution.py
+++ b/solution.py
@@ -26,7 +26,7 @@
     gate_f, up_f, gate_grad, up_grad, part, part_recv, middle, sums, sums_recv, grad_out,
     out_send, out_recv, early,
     w_s, w_r, h_s, h_r, u1_s, u1_r, u2_s, u2_r, g1_s, g1_r, g2_s, g2_r,
-    a_s, a_r, b_s, b_r, x_s, x_r, o_s, o_r,
+    a_s, a_r, b_s, b_r, x_s, x_r, o_s, o_r, l_s,
 ):
     sections, experts, n_dp, chunks, rows, tok, width = sizes
     sec = lax.axis_index("pipe")
@@ -127,7 +127,7 @@
         for i in range(1, n_dp):
             d, where = other(i)
             copy(ref, weights.at[k, core], w_s.at[k, d], w_r.at[k, core], where).start()
-        weights[k, core] = ref[...]
+        pltpu.make_async_copy(ref, weights.at[k, core], l_s.at[k]).start()
 
     @pl.when(sec == last)
     def _():
@@ -154,6 +154,7 @@
         for i in range(1, n_dp):
             d, where = other(i)
             copy(ref, weights.at[k, d], w_s.at[k, d], w_r.at[k, d], where).wait_recv()
+        pltpu.make_async_copy(ref, weights.at[k, core], l_s.at[k]).wait()
 
     per_block = GROUP if GROUP * experts * rows <= 256 else 1
     blocks = [(first, per_block) for first in range(0, GROUP, per_block)]
@@ -175,6 +176,10 @@
             at = pl.ds(c * GROUP * experts * rows + first * experts * rows, block_rows)
             gate_f[at, :] = project(x, 0)
             up_f[at, :] = project(x, 1)
+
+        @pl.when(sec == last)
+        def _():
+            relay(c, grad_full, g2_s, g2_r)
 
     def backward(c):
         spread_end(c, grad_full, g2_s, g2_r)
@@ -263,9 +268,9 @@
                 spread_one(t + 3, grad_in[t + 3], grad_send, grad_full, g1_s, g1_r)
             if 0 <= t + 2 < chunks:
                 spread_two(t + 2, grad_send, grad_full, g1_s, g1_r, g2_s, g2_r)
-
-        if 0 <= t + 1 < chunks:
-            relay(t + 1, grad_full, g2_s, g2_r)
+            if 0 <= t + 1 < chunks:
+                relay(t + 1, grad_full, g2_s, g2_r)
+
         if 0 <= t < chunks:
             if t > 0 and t == chunks - 1:
                 pl.when(sec == 0)(sum_early)
@@ -378,13 +383,13 @@
         dma((chunks, 6)), dma((chunks, 6)),
         dma((chunks, experts)), dma((chunks, experts)),
         dma((chunks,)), dma((chunks,)),
-        dma((2, n_dp)), dma((2, n_dp)),
+        dma((2, n_dp)), dma((2, n_dp)), dma((3,)),
     ]
     flops = 14 * all_rows * hidden * width
     gate, up = pl.pallas_call(
         functools.partial(kernel, sizes),
         out_shape=(result, result),
-        in_specs=[pl.BlockSpec(memory_space=pltpu.VMEM)] * 6,
+        in_specs=[pl.BlockSpec(memory_space=pltpu.VMEM)] * 3 + [pl.BlockSpec(memory_space=pl.ANY)] * 3,
         out_specs=[pl.BlockSpec(memory_space=pltpu.VMEM)] * 2,
         scratch_shapes=scratch,
         compiler_params=pltpu.CompilerParams(

time: 141 us -> 141 us (level)
  no operation moved by 1% of the time
where the time goes in v4:
time: 141 us
  Pallas kernels  137 us (97%)
  local copies, waits for them, and re-layouts  3.4 us (2%)
    pallas_call x1, Pallas kernels, shards(): pl.pallas_call(functools.partial(kernel, sizes), out_shape=(result, resul...  137 us
    unnamed x6, local copies, waits for them, and re-layouts  3.29 us

profile of v4, /device:TPU:1, one launch (start us, length us, event | category | flops | bytes accessed | tf_op | source)
XLA Modules:
  0.0 141.1 jit_solution(11368847020778334126)
XLA Ops:
  0.6 0.0 copy-start.1
  0.6 0.6 copy-done.1
  1.3 0.1 copy.8.routes
  1.4 0.0 copy-start
  1.4 1.0 copy-done
  2.4 137.0 %shard_map.77 = (bf16[256,1280]{1,0:T(8,128)(2,1)S(1)}, bf16[256,1280]{1,0:T(8,128)(2,1)S(1)}) custom-call(bf16[128,2560]{1,0:T(8,128)(2,1)} %bitcast.10, bf16[128,1280]{1,0:T(8,128)(2,1)S(1)} %copy-done, s32[128,1]{1,0:T(8,128)S(1)} %copy.8.routes, bf16[256,1280]{1,0:T(8,128)(2,1)} %bitcast.11, bf16[256,1280]{1,0:T(8,128)(2,1)} %bitcast.12, ...), custom_call_target="tpu_custom_call" | custom-call | flops 4697620480 | bytes 3932160 | tf_op jit(solution)/shard_map/pallas_call | solution.py:389
  139.4 0.8 copy.11
  140.2 0.8 copy.12
Async XLA Ops:
  0.6 0.7 copy-start.1
  1.4 1.0 copy-start

commit v5 on v3

--- a/solution.py
+++ b/solution.py
@@ -253,7 +253,7 @@
     def sum_early():
         for k in range(2):
             for d in range(n_dp):
-                early[k, d] = outer(k, d, 0, chunks - 1)
+                early[k, d] = outer(k, d, 0, chunks // 2)
 
     for t in range(-3, chunks + 3):
         @pl.when(sec != last)
@@ -267,7 +267,7 @@
         if 0 <= t + 1 < chunks:
             relay(t + 1, grad_full, g2_s, g2_r)
         if 0 <= t < chunks:
-            if t > 0 and t == chunks - 1:
+            if t > 0 and t == max(chunks - 2, chunks // 2):
                 pl.when(sec == 0)(sum_early)
             backward(t)
 
@@ -289,7 +289,7 @@
                     o_s.at[k, d], o_r.at[k, core if mine else d], where)
 
     def outer_all(k, d):
-        value = outer(k, d, chunks - 1, 1)
+        value = outer(k, d, chunks // 2, chunks - chunks // 2)
         if chunks > 1:
             value = value + early[k, d]
         out_send[k, d] = value.astype(BF16)

time: 141 us -> 141 us (level)
  no operation moved by 1% of the time
where the time goes in v5:
time: 141 us
  Pallas kernels  137 us (97%)
  local copies, waits for them, and re-layouts  3.4 us (2%)
    pallas_call x1, Pallas kernels, shards(): pl.pallas_call(functools.partial(kernel, sizes), out_shape=(result, resul...  137 us
    unnamed x6, local copies, waits for them, and re-layouts  3.29 us

profile of v5, /device:TPU:1, one launch (start us, length us, event | category | flops | bytes accessed | tf_op | source)
XLA Modules:
  0.0 140.9 jit_solution(8425131875830112480)
XLA Ops:
  0.6 0.0 copy-start.1
  0.6 0.6 copy-done.1
  1.3 0.1 copy.8.routes
  1.4 0.0 copy-start
  1.4 1.0 copy-done
  2.4 136.8 %shard_map.77 = (bf16[256,1280]{1,0:T(8,128)(2,1)S(1)}, bf16[256,1280]{1,0:T(8,128)(2,1)S(1)}) custom-call(bf16[128,2560]{1,0:T(8,128)(2,1)} %bitcast.10, bf16[128,1280]{1,0:T(8,128)(2,1)S(1)} %copy-done, s32[128,1]{1,0:T(8,128)S(1)} %copy.8.routes, bf16[256,1280]{1,0:T(8,128)(2,1)} %bitcast.11, bf16[256,1280]{1,0:T(8,128)(2,1)} %bitcast.12, ...), custom_call_target="tpu_custom_call" | custom-call | flops 4697620480 | bytes 3932160 | tf_op jit(solution)/shard_map/pallas_call | solution.py:384
  139.2 0.8 copy.11
  140.1 0.8 copy.12
Async XLA Ops:
  0.6 0.7 copy-start.1
  1.4 1.0 copy-start
